TPU v7x, 128 devices: a whole 4x4x4 slice. The times are simulated.
128 devices in a mesh: outer: 16 (over z, y_lo, core), inner: 8 (over x, y_hi).
Axes of the slice: x: 4, y: 4 (y_hi: 2, y_lo: 2; y = y_hi * 2 + y_lo), z: 4, core: 2. Of those that a mesh axis runs over, the one named last changes fastest.
Arguments:
- params: bfloat16 [8, 1536, 512], P('inner', 'outer'), may hold values from -0.0546875 to 0.0546875
- moment: bfloat16 [8, 1536, 512], P('inner', 'outer'), may hold values from -6 to 6
- second: bfloat16 [8, 1536, 512], P('inner', 'outer'), may hold values from 0.0099487305 to 4
- grad_prev: float32 [8, 1536, 512], P('inner', 'outer'), may hold values from -6 to 6
- tokens: bfloat16 [49152, 12288], P(('outer', 'inner')), may hold values from -24 to 24
- cotangent: bfloat16 [49152, 12288], P(('outer', 'inner')), may hold values from -0.109375 to 0.109375
Outputs:
- fresh: bfloat16 [8, 1536, 512], P('inner', 'outer')
- moment_new: bfloat16 [8, 1536, 512], P('inner', 'outer')
- second_new: bfloat16 [8, 1536, 512], P('inner', 'outer')
- gradient: float32 [8, 1536, 512], P('inner', 'outer')
All inputs are finite; a program needn't handle non-finite values.
Results may differ from a plain program's by a relative error of at most 0.0054.
Values may be sent and summed in bfloat16 or wider, within the bound.
A program may use at most 192 MiB of HBM per device.

v0:
```python
import jax
import jax.numpy as jnp
from jax import lax
from jax.sharding import PartitionSpec as P

beta_one = 0.9
beta_two = 0.95
bias_one = 0.9999734386011124
bias_two = 0.994079470779666
epsilon_adam = 1e-08
learn_rate = 6e-05
decay_rate = 0.1
root_scale = 0.7978845608028654
cubic_term = 0.044715


def gelu_pair(values):
    tangent = jnp.tanh(root_scale * (values + cubic_term * values * values * values))
    output = 0.5 * values * (1.0 + tangent)
    slope = 0.5 * (1.0 + tangent) + 0.5 * values * (1.0 - tangent * tangent) * root_scale * (
        1.0 + 3.0 * cubic_term * values * values
    )
    return (output, slope)


def adam_update(params, moment, second, grad_prev):
    moment_new = beta_one * moment.astype(jnp.float32) + (1.0 - beta_one) * grad_prev
    second_new = beta_two * second.astype(jnp.float32) + (1.0 - beta_two) * grad_prev * grad_prev
    update = moment_new / bias_one / (
        jnp.sqrt(second_new / bias_two) + epsilon_adam
    ) + decay_rate * params.astype(jnp.float32)
    fresh = params.astype(jnp.float32) - learn_rate * update
    return (
        fresh.astype(jnp.bfloat16),
        moment_new.astype(jnp.bfloat16),
        second_new.astype(jnp.bfloat16),
    )


def reorder(array, inner_count, outer_count):
    rows_here, width = array.shape
    block = width // (inner_count * outer_count)
    shaped = array.reshape(rows_here, inner_count, outer_count, block)
    return shaped.transpose(0, 2, 1, 3).reshape(rows_here, width)


def per_device(params, moment, second, grad_prev, tokens, cotangent):
    fresh, moment_new, second_new = adam_update(params, moment, second, grad_prev)
    partition = lax.all_gather(fresh, "outer", axis=1, tiled=True)
    slab = partition[0]
    hidden_width = slab.shape[1] // 2
    piece = lax.all_gather(slab, "inner", axis=0, tiled=True)
    first = jnp.dot(tokens, piece[:, :hidden_width], preferred_element_type=jnp.float32)
    other = jnp.dot(cotangent, piece[:, hidden_width:], preferred_element_type=jnp.float32)
    preact = first
    backward = other
    activ, slope = gelu_pair(preact)
    hidden = activ.astype(jnp.bfloat16)
    delta = (backward * slope).astype(jnp.bfloat16)
    contract = (((0,), (0,)), ((), ()))

    def term_rows(source_tok, source_cot):

        def compute(offset, length):
            first = lax.dot_general(source_tok, delta, contract, preferred_element_type=jnp.float32)
            other = lax.dot_general(
                source_cot, hidden, contract, preferred_element_type=jnp.float32
            )
            return jnp.concatenate([first, other], axis=1)

        return compute

    width = tokens.shape[1]
    inner_count = lax.axis_size("inner")
    outer_count = lax.axis_size("outer")
    compute = term_rows(
        reorder(tokens, inner_count, outer_count), reorder(cotangent, inner_count, outer_count)
    )
    shard = lax.psum_scatter(
        compute(
            jnp.int32(0), width // (inner_count * outer_count) * lax.axis_size(("outer", "inner"))
        ),
        ("outer", "inner"),
        scatter_dimension=0,
        tiled=True,
    )
    return (fresh, moment_new, second_new, shard[None])


def solution(mesh):
    in_specs = (
        P("inner", "outer", None),
        P("inner", "outer", None),
        P("inner", "outer", None),
        P("inner", "outer", None),
        P(("outer", "inner"), None),
        P(("outer", "inner"), None),
    )
    out_specs = (
        P("inner", "outer", None),
        P("inner", "outer", None),
        P("inner", "outer", None),
        P("inner", "outer", None),
    )
    return jax.shard_map(
        per_device, mesh=mesh, in_specs=in_specs, out_specs=out_specs, check_vma=False
    )
```

profile of v0, /device:TPU:1, one launch (start us, length us, event | category | flops | bytes accessed | tf_op | source)
XLA Modules:
  0.0 985.2 jit_solution(4831162854566299089)
XLA Ops:
  7.2 0.0 all-gather.4.cloned.1.call-start
  7.2 2.0 fusion.30
  9.2 0.0 all-gather.4.cloned.1.call-update
  9.2 0.0 all-gather.6.cloned.1.call-start
  9.3 37.9 %all-gather.4.cloned.1.call-done = bf16[1,1536,512]{2,1,0:T(8,128)(2,1)} async-done(((bf16[1,96,512]{2,1,0:T(8,128)(2,1)}), bf16[1,1536,512]{2,1,0:T(8,128)(2,1)}) %all-gather.4.cloned.1.call-update) | async-done | bytes 1572880 | tf_op jit(solution)/shard_map/all_gather | solution.py:49
  47.2 0.0 all-gather.6.cloned.1.call-update
  47.2 0.0 reduce-scatter.4.cloned.1.call-start
  47.3 12.7 %copy.16 = bf16[384,12288]{0,1:T(8,128)(2,1)} copy(bf16[384,12288]{1,0:T(8,128)(2,1)} %param.10) | data formatting | bytes 18874368 | tf_op args[4]
  60.0 9.6 copy.17
  69.6 12.6 %copy.18 = bf16[384,12288]{0,1:T(8,128)(2,1)} copy(bf16[384,12288]{1,0:T(8,128)(2,1)} %param.11) | data formatting | bytes 18874368 | tf_op args[5]
  82.2 9.1 copy.19
  91.3 104.9 %all-gather.6.cloned.1.call-done = bf16[1,12288,512]{2,1,0:T(8,128)(2,1)} async-done(((bf16[1,1536,512]{2,1,0:T(8,128)(2,1)}), bf16[1,12288,512]{2,1,0:T(8,128)(2,1)}) %all-gather.6.cloned.1.call-update) | async-done | bytes 12582928 | tf_op jit(solution)/shard_map/all_gather | solution.py:52
  196.2 0.0 copy-start
  196.2 10.6 %fusion.10 = f32[384,256]{0,1:T(8,128)S(1)} fusion(bf16[384,12288]{1,0:T(8,128)(2,1)} %param.10, bf16[12288,512]{1,0:T(8,128)(2,1)} %bitcast.33), kind=kOutput, calls=%fused_computation.9 | convolution fusion | flops 2415919104 | bytes 16121856 | tf_op jit(solution)/shard_map/dot_general | solution.py:53
  206.8 0.0 copy-done
  206.8 7.2 fusion.13
  214.0 6.1 convolution_bitcast_fusion
  220.1 12.5 %convolution_bitcast_fusion.1 = f32[12288,256]{0,1:T(8,128)} fusion(bf16[384,256]{0,1:T(8,128)(2,1)S(1)} %fusion.13, bf16[384,12288]{0,1:T(8,128)(2,1)} %bitcast.30), kind=kOutput, calls=%fused_computation.2 | convolution fusion | flops 2415919104 | bytes 22216704 | tf_op jit(solution)/shard_map/dot_general | solution.py:65
  232.6 14.0 %pad_maximum_fusion = f32[12288,512]{0,1:T(8,128)} fusion(f32[12288,256]{0,1:T(8,128)S(1)} %convolution_bitcast_fusion, f32[12288,256]{0,1:T(8,128)} %convolution_bitcast_fusion.1), kind=kLoop, calls=%fused_computation | loop fusion | flops 6291456 | bytes 50331648 | tf_op jit(solution)/shard_map/concatenate | solution.py:69
  246.6 24.6 %copy.21 = f32[12288,512]{1,0:T(8,128)} copy(f32[12288,512]{0,1:T(8,128)} %pad_maximum_fusion) | data formatting | bytes 50331648
  271.3 0.0 reduce-scatter.4.cloned.1.call-update
  271.3 705.5 %reduce-scatter.4.cloned.1.call-done = f32[96,512]{1,0:T(8,128)} async-done(((f32[12288,512]{1,0:T(8,128)}), f32[96,512]{1,0:T(8,128)}) %reduce-scatter.4.cloned.1.call-update) | async-done | bytes 196624
  976.8 1.0 copy.22
  977.9 0.8 copy.20
Async XLA Ops:
  7.2 40.1 %all-gather.4.cloned.1.call-start = ((), (), s32[]{:S(2)}) async-start(), calls=%async_computation.1 | async-start | bytes 1671168 | tf_op jit(solution)/shard_map/all_gather | solution.py:49
  9.2 186.9 %all-gather.6.cloned.1.call-start = ((), (), s32[]{:S(2)}) async-start(), calls=%async_computation.2 | async-start | bytes 14155776 | tf_op jit(solution)/shard_map/all_gather | solution.py:52
  47.2 929.6 %reduce-scatter.4.cloned.1.call-start = ((), (), s32[]{:S(2)}) async-start(), calls=%async_computation.3 | async-start | bytes 25362432
  196.2 10.6 %copy-start = (bf16[1,12288,512]{2,1,0:T(8,128)(2,1)S(1)}, bf16[1,12288,512]{2,1,0:T(8,128)(2,1)}, u32[]{:S(2)}) copy-start(bf16[1,12288,512]{2,1,0:T(8,128)(2,1)} %all-gather.6.cloned.1.call-done) | copy-start | bytes 37748740
Sparse Core Ops, SparseCore 0:
  10.3 36.9 all-gather.3
  49.5 146.5 all-gather.5
  271.4 705.3 reduce-scatter.3
where the time goes:
time: 994 us; the launch traced here: 985 us
  waiting for transfers between devices  848 us (85%)
  local copies, waits for them, and re-layouts  70.5 us (7%)
  matrix products  36.4 us (4%)
  other arithmetic  16 us (2%)
  between operations  13.8 us (1%)
    unnamed x4, waiting for transfers between devices  706 us
    all_gather x1, waiting for transfers between devices, per_device(): piece = lax.all_gather(slab, 'inner', axis=0, tiled=True)  105 us
    unnamed x7, local copies, waits for them, and re-layouts  51.8 us
    all_gather x1, waiting for transfers between devices, per_device(): partition = lax.all_gather(fresh, 'outer', axis=1, tiled=True)  37.9 us
  transfers between devices with their start and end apart: 3, of which 3 were waited for; matrix products, arithmetic and copies ran while one was open for 4% of the time, Pallas kernels for 0%

commit v1 on v0

v1 whole, which is shorter than its diff:
```python
import functools

import jax
import jax.numpy as jnp
from jax import lax
from jax.experimental import pallas as pl
from jax.experimental.pallas import tpu as pltpu
from jax.sharding import PartitionSpec as P

beta_one = 0.9
beta_two = 0.95
bias_one = 0.9999734386011124
bias_two = 0.994079470779666
epsilon_adam = 1e-08
learn_rate = 6e-05
decay_rate = 0.1
root_scale = 0.7978845608028654
cubic_term = 0.044715

MESH = pl.DeviceIdType.MESH
f32 = jnp.float32
bf16 = jnp.bfloat16

ORDER = ((0, 1, 2), (1, 2, 0), (2, 0, 1))
STEPS = (2, 1, -1, 0)
SLOT = {2: 0, 1: 1, -1: 2, 0: 3}
WAYS = (1, -1)
SIDE = {1: 0, -1: 1}


def gelu_value(values):
    tangent = jnp.tanh(root_scale * (values + cubic_term * values * values * values))
    return 0.5 * values * (1.0 + tangent)


def gelu_slope(values):
    tangent = jnp.tanh(root_scale * (values + cubic_term * values * values * values))
    return 0.5 * (1.0 + tangent) + 0.5 * values * (1.0 - tangent * tangent) * root_scale * (
        1.0 + 3.0 * cubic_term * values * values
    )


def adam_update(params, moment, second, grad_prev):
    moment_new = beta_one * moment.astype(f32) + (1.0 - beta_one) * grad_prev
    second_new = beta_two * second.astype(f32) + (1.0 - beta_two) * grad_prev * grad_prev
    update = moment_new / bias_one / (
        jnp.sqrt(second_new / bias_two) + epsilon_adam
    ) + decay_rate * params.astype(f32)
    fresh = params.astype(f32) - learn_rate * update
    return (fresh.astype(bf16), moment_new.astype(bf16), second_new.astype(bf16))


def ring(place, step):
    return lax.rem(place + (step + 4), 4)


def device(x, y, z, core):
    return {"outer": z * 4 + lax.rem(y, 2) * 2 + core, "inner": x * 2 + y // 2}


def kernel(
    params, moment, second, grad_prev, tokens, cotangent,
    fresh_out, moment_out, second_out, gradient_out,
    act, held, grads, acc, other, turned, stage,
    first_rows, full_rows, full_units, first_second, second_units, first_last, last_unit,
    final, finals, send_sems, recv_sems, local_sems,
):
    outer = lax.axis_index("outer")
    inner = lax.axis_index("inner")
    core = lax.rem(outer, 2)
    y_lo = lax.rem(outer // 2, 2)
    own = (inner // 2, lax.rem(inner, 2) * 2 + y_lo, outer // 4)

    def neighbour(axis, way):
        place = list(own)
        place[axis] = ring(place[axis], way)
        return device(*place, core)

    def partner(which):
        return device(
            own[0], own[1] - y_lo + lax.rem(y_lo + which // 2, 2), own[2], lax.rem(core + which % 2, 2)
        )

    neighbours = {(axis, way): neighbour(axis, way) for axis in range(3) for way in WAYS}
    sibling = partner(1)

    barrier = pltpu.get_barrier_semaphore()
    greeted = list(neighbours.values()) + [sibling, partner(3)]
    for one in greeted:
        pl.semaphore_signal(barrier, inc=1, device_id=one, device_id_type=MESH)

    mine = pl.ds(pl.multiple_of(core * 384, 384), 384)

    def load_own(source):
        return pltpu.make_async_copy(source, act.at[mine], local_sems.at[0])

    @pl.when(core == 0)
    def _():
        load_own(tokens).start()

    @pl.when(core == 1)
    def _():
        load_own(cotangent).start()

    messages = {}

    def send(key, source, target, to):
        index = len(messages)
        copy = pltpu.make_async_remote_copy(
            src_ref=source,
            dst_ref=target,
            send_sem=send_sems.at[index],
            recv_sem=recv_sems.at[index],
            device_id=to,
            device_id_type=MESH,
        )
        messages[key] = copy
        copy.start()

    def arrived(key):
        messages[key].wait_recv()

    fresh, moment_new, second_new = adam_update(params[0], moment[0], second[0], grad_prev[0])
    fresh_out[0] = fresh
    moment_out[0] = moment_new
    second_out[0] = second_new
    stage[0] = fresh[:, :256]
    stage[1] = fresh[:, 256:]

    pl.semaphore_wait(barrier, len(greeted))

    send("rows", stage.at[1 - core], stage.at[2], sibling)

    def load_sibling(source):
        return pltpu.make_async_remote_copy(
            src_ref=source,
            dst_ref=act.at[mine],
            send_sem=local_sems.at[1],
            recv_sem=local_sems.at[2],
            device_id=sibling,
            device_id_type=MESH,
        )

    @pl.when(core == 0)
    def _():
        load_sibling(cotangent).start()

    @pl.when(core == 1)
    def _():
        load_sibling(tokens).start()

    def places(p):
        return tuple(own[axis] for axis in ORDER[p])

    arrived("rows")
    for first_core in range(2):
        @pl.when(core == first_core)
        def _():
            low, high = (stage[first_core], stage[2]) if first_core == 0 else (stage[2], stage[first_core])
            pieces = (low[:64], jnp.concatenate([low[64:], high[:32]], axis=0), high[32:])
            for p in range(3):
                one, two, three = places(p)
                held[p, three, two, one] = pieces[p]

    def half(way, rows):
        return pl.ds(SIDE[way] * (rows // 2), rows // 2)

    def unit(p, three, two, one):
        return held.at[p, three, two, one]

    def give(key, p, level, ref):
        for way in WAYS:
            send((key[0], p, way) + key[1:], ref, ref, neighbours[ORDER[p][level], way])

    def pass_on(key, p, level, way, ref):
        send(key, ref, ref, neighbours[ORDER[p][level], way])

    for p in range(3):
        one, two, three = places(p)
        give(("g1",), p, 0, unit(p, three, two, one))
    for p in range(3):
        one, two, three = places(p)
        give(("g2", 0), p, 1, unit(p, three, two, one))
    for p in range(3):
        one, two, three = places(p)
        give(("g3", 0), p, 2, unit(p, three, two, one))
    for p in range(3):
        one, two, three = places(p)
        for way in WAYS:
            arrived(("g1", p, way))
            pass_on(("g1f", p, way), p, 0, way, held.at[p, three, two, ring(one, -way), half(way, 64)])
    for p in range(3):
        one, two, three = places(p)
        for step in WAYS:
            give(("g2", step), p, 1, unit(p, three, two, ring(one, step)))
    for p in range(3):
        one, two, three = places(p)
        for step in WAYS:
            give(("g3", step), p, 2, unit(p, three, two, ring(one, step)))

    def pass_second(p, step):
        one, two, three = places(p)
        for way in WAYS:
            arrived(("g2", p, way, step))
            pass_on(
                ("g2f", p, way, step), p, 1, way,
                held.at[p, three, ring(two, -way), ring(one, step), half(way, 64)],
            )

    for p in range(3):
        pass_second(p, 0)
    for p in range(3):
        one, two, three = places(p)
        for way in WAYS:
            arrived(("g1f", p, way))
        give(("g2", 2), p, 1, unit(p, three, two, ring(one, 2)))
        give(("g3", 2), p, 2, unit(p, three, two, ring(one, 2)))
    for p in range(3):
        for step in WAYS:
            pass_second(p, step)
    for p in range(3):
        pass_second(p, 2)
        one, two, three = places(p)
        for step in WAYS:
            give(("g3r", step), p, 2, held.at[p, three, ring(two, step)])
    for p in range(3):
        one, two, three = places(p)
        for way in WAYS:
            for step in STEPS:
                arrived(("g2f", p, way, step))
        give(("g3r", 2), p, 2, held.at[p, three, ring(two, 2)])

    def pass_third(p, step):
        one, two, three = places(p)
        for way in WAYS:
            if step == 0:
                for k in STEPS:
                    arrived(("g3", p, way, k))
            else:
                arrived(("g3r", p, way, step))
            pass_on(
                ("g3f", p, way, step), p, 2, way,
                held.at[p, ring(three, -way), ring(two, step), :, half(way, 64)],
            )

    for step in (0, 1, -1, 2):
        for p in range(3):
            pass_third(p, step)
    load_own(tokens).wait()
    load_sibling(tokens).wait()
    for step in (0, 1, -1, 2):
        for p in range(3):
            for way in WAYS:
                arrived(("g3f", p, way, step))

    def block(p, x, y, z):
        place = (x, y, z)
        return tuple(place[axis] for axis in reversed(ORDER[p]))

    def weight_rows(x, y_hi, z):
        return [
            held[(p,) + block(p, x, y_hi * 2 + low, z)] for low in range(2) for p in range(3)
        ]

    def product(step, carry):
        x, y_hi = step // 2, lax.rem(step, 2)
        rows = []
        for z in range(4):
            rows += weight_rows(x, y_hi, z)
        columns = pl.ds(pl.multiple_of(step * 1536, 1536), 1536)
        part = jnp.dot(act[:, columns], jnp.concatenate(rows, axis=0), preferred_element_type=f32)

        @pl.when(step == 0)
        def _():
            acc[...] = part

        @pl.when(step > 0)
        def _():
            acc[...] += part

        return carry

    lax.fori_loop(0, 8, product, 0)

    send("products", acc, other, sibling)
    arrived("products")
    for rows in range(3):
        span = slice(rows * 256, (rows + 1) * 256)

        @pl.when(core == 0)
        def _():
            turned[:, span] = (other[span] * gelu_slope(acc[span])).T.astype(bf16)

        @pl.when(core == 1)
        def _():
            turned[:, span] = gelu_value(other[span]).T.astype(bf16)

    def terms(step, carry):
        x, y_hi, z_hi = step // 4, lax.rem(step // 2, 2), lax.rem(step, 2)
        columns = pl.ds(pl.multiple_of(step * 768, 768), 768)
        part = jnp.dot(turned[...], act[:, columns], preferred_element_type=f32).astype(bf16)
        for z_lo in range(2):
            for p in range(3):
                for low in range(2):
                    start = (z_lo * 3 + p) * 128
                    grads[(p,) + block(p, x, y_hi * 2 + low, z_hi * 2 + z_lo)] = part[
                        low * 128 : low * 128 + 128, start : start + 128
                    ]
        return carry

    lax.fori_loop(0, 16, terms, 0)

    for step in STEPS:
        for p in range(3):
            one, two, three = places(p)
            for way in WAYS:
                send(
                    ("s1", p, way, step),
                    grads.at[p, ring(three, 2), ring(two, step), :, half(way, 128)],
                    first_rows.at[p, SIDE[way], SLOT[step]],
                    neighbours[ORDER[p][2], way],
                )

    def add_first(p, way, step):
        one, two, three = places(p)
        arrived(("s1", p, way, step))
        ref = grads.at[p, ring(three, way), ring(two, step), :, half(way, 128)]
        ref[...] = (ref[...].astype(f32) + first_rows[p, SIDE[way], SLOT[step]].astype(f32)).astype(bf16)

    for step in (2, 1, -1):
        for p in range(3):
            one, two, three = places(p)
            for way in WAYS:
                add_first(p, way, step)
                send(
                    ("s2", p, way, step),
                    grads.at[p, ring(three, way), ring(two, step)],
                    full_rows.at[p, SIDE[way], SLOT[step]],
                    neighbours[ORDER[p][2], way],
                )

    def send_own_row(p, way, step):
        one, two, three = places(p)
        send(
            ("s2u", p, way, step),
            grads.at[p, ring(three, way), two, ring(one, step)],
            full_units.at[p, SIDE[way], SLOT[step]],
            neighbours[ORDER[p][2], way],
        )

    for p in range(3):
        for way in WAYS:
            add_first(p, way, 0)
            send_own_row(p, way, 2)

    def sum_row(p, step):
        one, two, three = places(p)
        for way in WAYS:
            arrived(("s2", p, way, step))
        return (
            grads[p, three, ring(two, step)].astype(f32)
            + full_rows[p, 0, SLOT[step]].astype(f32)
            + full_rows[p, 1, SLOT[step]].astype(f32)
        )

    for p in range(3):
        one, two, three = places(p)
        grads[p, three, ring(two, 2)] = sum_row(p, 2).astype(bf16)
        for way in WAYS:
            send(
                ("s3", p, way),
                grads.at[p, three, ring(two, 2), :, half(way, 128)],
                first_second.at[p, SIDE[way]],
                neighbours[ORDER[p][1], way],
            )
    for step in WAYS:
        for p in range(3):
            for way in WAYS:
                send_own_row(p, way, step)

    for p in range(3):
        one, two, three = places(p)
        for way in WAYS:
            row = sum_row(p, way)
            arrived(("s3", p, way))
            low, high = row[:, :64], row[:, 64:]
            extra = first_second[p, SIDE[way]].astype(f32)
            low, high = (low + extra, high) if way == 1 else (low, high + extra)
            grads[p, three, ring(two, way), :, :64] = low.astype(bf16)
            grads[p, three, ring(two, way), :, 64:] = high.astype(bf16)
        for step in (2, 1, -1):
            for way in WAYS:
                send(
                    ("s4", p, way, step),
                    grads.at[p, three, ring(two, way), ring(one, step)],
                    second_units.at[p, SIDE[way], SLOT[step]],
                    neighbours[ORDER[p][1], way],
                )
    for p in range(3):
        one, two, three = places(p)
        for way in WAYS:
            send_own_row(p, way, 0)

    def sum_unit(p, step):
        one, two, three = places(p)
        total = grads[p, three, two, ring(one, step)].astype(f32)
        for way in WAYS:
            arrived(("s2u", p, way, step))
            total += full_units[p, SIDE[way], SLOT[step]].astype(f32)
        for way in WAYS:
            arrived(("s4", p, way, step))
            total += second_units[p, SIDE[way], SLOT[step]].astype(f32)
        return total

    for p in range(3):
        one, two, three = places(p)
        grads[p, three, two, ring(one, 2)] = sum_unit(p, 2).astype(bf16)
        for way in WAYS:
            send(
                ("s5", p, way),
                grads.at[p, three, two, ring(one, 2), half(way, 128)],
                first_last.at[p, SIDE[way]],
                neighbours[ORDER[p][0], way],
            )
    for p in range(3):
        one, two, three = places(p)
        for way in WAYS:
            send(
                ("s4", p, way, 0),
                grads.at[p, three, ring(two, way), one],
                second_units.at[p, SIDE[way], SLOT[0]],
                neighbours[ORDER[p][1], way],
            )
    for p in range(3):
        one, two, three = places(p)
        for way in WAYS:
            total = sum_unit(p, way)
            arrived(("s5", p, way))
            low, high = total[:64], total[64:]
            extra = first_last[p, SIDE[way]].astype(f32)
            low, high = (low + extra, high) if way == 1 else (low, high + extra)
            grads[p, three, two, ring(one, way), :64] = low.astype(bf16)
            grads[p, three, two, ring(one, way), 64:] = high.astype(bf16)
            send(
                ("s6", p, way),
                grads.at[p, three, two, ring(one, way)],
                last_unit.at[p, SIDE[way]],
                neighbours[ORDER[p][0], way],
            )
    for p in range(3):
        total = sum_unit(p, 0)
        for way in WAYS:
            arrived(("s6", p, way))
            total += last_unit[p, SIDE[way]].astype(f32)
        final[p * 128 : p * 128 + 128] = total.T

    index = y_lo * 2 + core
    for which in (3, 2, 1):
        to = lax.rem(y_lo + which // 2, 2) * 2 + lax.rem(core + which % 2, 2)
        send(
            ("end", which),
            final.at[pl.ds(pl.multiple_of(to * 96, 96), 96)],
            finals.at[index],
            partner(which),
        )
    finals[index] = final[pl.ds(pl.multiple_of(index * 96, 96), 96)]
    for which in (1, 2, 3):
        arrived(("end", which))
    for source in range(4):
        start = (source % 2) * 256 + (source // 2) * 128
        gradient_out[0, :, start : start + 128] = finals[source]

    for copy in messages.values():
        copy.wait_send()


def per_device(params, moment, second, grad_prev, tokens, cotangent):
    vmem = pl.BlockSpec(memory_space=pltpu.VMEM)
    shard = (1, 96, 512)
    n_messages = 300
    return pl.pallas_call(
        kernel,
        out_shape=(
            jax.ShapeDtypeStruct(shard, bf16),
            jax.ShapeDtypeStruct(shard, bf16),
            jax.ShapeDtypeStruct(shard, bf16),
            jax.ShapeDtypeStruct(shard, f32),
        ),
        in_specs=[vmem] * 4 + [pl.BlockSpec(memory_space=pl.ANY)] * 2,
        out_specs=(vmem,) * 4,
        scratch_shapes=[
            pltpu.VMEM((768, 12288), bf16),
            pltpu.VMEM((3, 4, 4, 4, 64, 256), bf16),
            pltpu.VMEM((3, 4, 4, 4, 128, 128), bf16),
            pltpu.VMEM((768, 256), f32),
            pltpu.VMEM((768, 256), f32),
            pltpu.VMEM((256, 768), bf16),
            pltpu.VMEM((3, 96, 256), bf16),
            pltpu.VMEM((3, 2, 4, 4, 64, 128), bf16),
            pltpu.VMEM((3, 2, 3, 4, 128, 128), bf16),
            pltpu.VMEM((3, 2, 4, 128, 128), bf16),
            pltpu.VMEM((3, 2, 4, 64, 128), bf16),
            pltpu.VMEM((3, 2, 4, 128, 128), bf16),
            pltpu.VMEM((3, 2, 64, 128), bf16),
            pltpu.VMEM((3, 2, 128, 128), bf16),
            pltpu.VMEM((384, 128), f32),
            pltpu.VMEM((4, 96, 128), f32),
            pltpu.SemaphoreType.DMA((n_messages,)),
            pltpu.SemaphoreType.DMA((n_messages,)),
            pltpu.SemaphoreType.DMA((3,)),
        ],
        compiler_params=pltpu.CompilerParams(
            collective_id=0, has_side_effects=True, vmem_limit_bytes=56 * 2**20
        ),
    )(params, moment, second, grad_prev, tokens, cotangent)


def solution(mesh):
    blocks = P("inner", "outer", None)
    rows = P(("outer", "inner"), None)
    return jax.shard_map(
        per_device,
        mesh=mesh,
        in_specs=(blocks,) * 4 + (rows,) * 2,
        out_specs=(blocks,) * 4,
        check_vma=False,
    )
```

time: 994 us -> 102 us (0.10)
  waiting for transfers between devices: 848 us -> 0 us
  Pallas kernels: 0 us -> 94.1 us
  local copies, waits for them, and re-layouts: 70.5 us -> 6.23 us
  matrix products: 36.4 us -> 0 us
  other arithmetic: 16 us -> 0 us
  between operations: 13.8 us -> 0.64 us
    unnamed x4 -> x0, waiting for transfers between devices: 706 us -> none
    all_gather x2 -> x0, waiting for transfers between devices: 143 us -> none  [the longest x1 105 us: per_device(): piece = lax.all_gather(slab, 'inner', axis=0, tiled=True)]
    pallas_call x0 -> x1, Pallas kernels: none -> 94.1 us  [per_device(): pl.pallas_call(kernel, out_shape=(jax.ShapeDtypeStruct(shard, bf16), jax....]
    unnamed x7 -> x4, local copies, waits for them, and re-layouts: 51.8 us -> 6.23 us
    dot_general x4 -> x0, matrix products: 36.4 us -> none  [the longest x1 12.5 us: compute(): lax.dot_general(source_tok, delta, contract, preferred_element_type=jnp.f...]
    transpose x2 -> x0, local copies, waits for them, and re-layouts: 18.7 us -> none  [reorder(): return shaped.transpose(0, 2, 1, 3).reshape(rows_here, width)]
    concatenate x1 -> x0, other arithmetic: 14 us -> none  [compute(): return jnp.concatenate([first, other], axis=1)]
  transfers between devices with their start and end apart: 3 -> 0, of which waited for: 3 -> 0; matrix products, arithmetic and copies ran while one was open for 4% -> 0% of each run, Pallas kernels for 0% -> 0%
where the time goes in v1:
time: 102 us; the launch traced here: 101 us
  Pallas kernels  94.1 us (92%)
  local copies, waits for them, and re-layouts  6.23 us (6%)
    pallas_call x1, Pallas kernels, per_device(): pl.pallas_call(kernel, out_shape=(jax.ShapeDtypeStruct(shard, bf16), jax....  94.1 us
    unnamed x4, local copies, waits for them, and re-layouts  6.23 us

profile of v1, /device:TPU:1, one launch (start us, length us, event | category | flops | bytes accessed | tf_op | source)
XLA Modules:
  0.0 100.9 jit_solution(3770513206742539572)
XLA Ops:
  0.6 94.1 %shard_map.93 = (bf16[1,96,512]{2,1,0:T(8,128)(2,1)}, bf16[1,96,512]{2,1,0:T(8,128)(2,1)}, bf16[1,96,512]{2,1,0:T(8,128)(2,1)}, f32[1,96,512]{2,1,0:T(8,128)}) custom-call(bf16[1,96,512]{2,1,0:T(8,128)(2,1)} %params.1, bf16[1,96,512]{2,1,0:T(8,128)(2,1)} %moment.1, bf16[1,96,512]{2,1,0:T(8,128)(2,1)} %second.1, f32[1,96,512]{2,1,0:T(8,128)} %grad_prev.1, ...), custom_call_target="tpu_custom_call" | custom-call | tf_op jit(solution)/shard_map/pallas_call | solution.py:481
  94.7 1.5 %copy.14 = bf16[1,96,512]{2,1,0:T(8,128)(2,1)} copy(bf16[1,96,512]{2,1,0:T(8,128)(2,1)} %get-tuple-element.8) | data formatting | bytes 196608
  96.2 1.5 %copy.15 = bf16[1,96,512]{2,1,0:T(8,128)(2,1)} copy(bf16[1,96,512]{2,1,0:T(8,128)(2,1)} %get-tuple-element.9) | data formatting | bytes 196608
  97.8 1.5 %copy.16 = bf16[1,96,512]{2,1,0:T(8,128)(2,1)} copy(bf16[1,96,512]{2,1,0:T(8,128)(2,1)} %get-tuple-element.10) | data formatting | bytes 196608
  99.3 1.6 %copy.17 = f32[1,96,512]{2,1,0:T(8,128)} copy(f32[1,96,512]{2,1,0:T(8,128)} %get-tuple-element.11) | data formatting | bytes 393216

commit v2 on v1

v2 whole, which is shorter than its diff:
```python
import functools

import jax
import jax.numpy as jnp
from jax import lax
from jax.experimental import pallas as pl
from jax.experimental.pallas import tpu as pltpu
from jax.sharding import PartitionSpec as P

beta_one = 0.9
beta_two = 0.95
bias_one = 0.9999734386011124
bias_two = 0.994079470779666
epsilon_adam = 1e-08
learn_rate = 6e-05
decay_rate = 0.1
root_scale = 0.7978845608028654
cubic_term = 0.044715

MESH = pl.DeviceIdType.MESH
f32 = jnp.float32
bf16 = jnp.bfloat16

ORDER = ((0, 1, 2), (1, 2, 0), (2, 0, 1))
STEPS = (2, 1, -1, 0)
SLOT = {2: 0, 1: 1, -1: 2, 0: 3}
WAYS = (1, -1)
SIDE = {1: 0, -1: 1}


def gelu_value(values):
    tangent = jnp.tanh(root_scale * (values + cubic_term * values * values * values))
    return 0.5 * values * (1.0 + tangent)


def gelu_slope(values):
    tangent = jnp.tanh(root_scale * (values + cubic_term * values * values * values))
    return 0.5 * (1.0 + tangent) + 0.5 * values * (1.0 - tangent * tangent) * root_scale * (
        1.0 + 3.0 * cubic_term * values * values
    )


def adam_update(params, moment, second, grad_prev):
    moment_new = beta_one * moment.astype(f32) + (1.0 - beta_one) * grad_prev
    second_new = beta_two * second.astype(f32) + (1.0 - beta_two) * grad_prev * grad_prev
    update = moment_new / bias_one / (
        jnp.sqrt(second_new / bias_two) + epsilon_adam
    ) + decay_rate * params.astype(f32)
    fresh = params.astype(f32) - learn_rate * update
    return (fresh.astype(bf16), moment_new.astype(bf16), second_new.astype(bf16))


def ring(place, step):
    return lax.rem(place + (step + 4), 4)


def device(x, y, z, core):
    return {"outer": z * 4 + lax.rem(y, 2) * 2 + core, "inner": x * 2 + y // 2}


GATHER = (
    *(("own", p, level) for level in range(3) for p in range(3)),
    *(step for p in range(3) for step in (("first", p), ("unit", p, 1, 1), ("unit", p, 1, -1))),
    *(("second", p, 0) for p in range(3)),
    *(("unit", p, 2, step) for p in range(3) for step in (1, -1)),
    *(("unit", p, 1, 2) for p in range(3)),
    *(("unit", p, 2, 2) for p in range(3)),
    *(("second", p, step) for p in range(3) for step in (1, -1)),
    *(("second", p, 2) for p in range(3)),
    *(("row", p, 1) for p in range(3)),
    *(("third", p, 0) for p in range(3)),
    *(("row", p, step) for p in range(3) for step in (2,)),
    *(("row", p, -1) for p in range(3)),
    *(("third", p, 1) for p in range(3)),
    *(("third", p, -1) for p in range(3)),
    ("mul", 0), ("mul", 1), ("mul", 2),
    *(("third", p, 2) for p in range(3)),
    ("mul", 3), ("mul", 4), ("mul", 5), ("mul", 6), ("mul", 7),
)
SCATTER = (
    ("terms", 0), ("first", 1, 2),
    ("terms", 1), ("first", 1, 1), ("first", 2, 2), ("first", 1, -1), ("first", 1, 0),
    ("terms", 2), ("first", 0, 2), ("first", 0, 1), ("first", 0, -1), ("first", 0, 0),
    ("terms", 3), ("first", 2, 1), ("terms", 4), ("first", 2, -1), ("terms", 5), ("first", 2, 0),
    *(("row", p, 2) for p in range(3)),
    *(("row", p, 1) for p in range(3)),
    *(step for p in range(3) for step in (("row", p, -1), ("second", p))),
    *(("own", p, 2) for p in range(3)),
    *(step for p in range(3) for step in (("add", p), ("unit", p, 2), ("unit", p, 1), ("unit", p, -1))),
    *(("own", p, step) for step in (1, -1) for p in range(3)),
    *(("third", p) for p in range(3)),
    *(("own", p, 0) for p in range(3)),
    *(("unit", p, 0) for p in range(3)),
    *(("last", p) for p in range(3)),
    *(("end", p) for p in range(3)),
)


def kernel(
    params, moment, second, grad_prev, tokens, cotangent,
    gradient_out,
    act, held, grads, acc, other, turned, stage,
    old_params, old_moment, old_second, old_grad,
    first_rows, full_rows, full_units, first_second, second_units, first_last, last_unit,
    final, finals, send_sems, recv_sems, local_sems,
):
    outer = lax.axis_index("outer")
    inner = lax.axis_index("inner")
    core = lax.rem(outer, 2)
    y_lo = lax.rem(outer // 2, 2)
    y_hi = lax.rem(inner, 2)
    own = (inner // 2, y_hi * 2 + y_lo, outer // 4)

    def neighbour(axis, way):
        place = list(own)
        place[axis] = ring(place[axis], way)
        return device(*place, core)

    def partner(which):
        return device(
            own[0], own[1] - y_lo + lax.rem(y_lo + which // 2, 2), own[2], lax.rem(core + which % 2, 2)
        )

    neighbours = {(axis, way): neighbour(axis, way) for axis in range(3) for way in WAYS}
    sibling = partner(1)

    barrier = pltpu.get_barrier_semaphore()
    greeted = list(neighbours.values()) + [sibling, partner(3)]
    for one in greeted:
        pl.semaphore_signal(barrier, inc=1, device_id=one, device_id_type=MESH)

    old = [
        pltpu.make_async_copy(source.at[0], target, local_sems.at[3 + index])
        for index, (source, target) in enumerate(
            ((params, old_params), (moment, old_moment), (second, old_second), (grad_prev, old_grad))
        )
    ]
    for copy in old:
        copy.start()

    mine = pl.ds(pl.multiple_of(core * 384, 384), 384)

    def load_own(source):
        return pltpu.make_async_copy(source, act.at[mine], local_sems.at[0])

    @pl.when(core == 0)
    def _():
        load_own(tokens).start()

    @pl.when(core == 1)
    def _():
        load_own(cotangent).start()

    groups = {}
    seen = set()
    leaving = {
        "rows": (0, stage.at[0]),
        "g1": (1, held.at[:, 0, 0, 0:3]), "g1f": (1,), "g2": (2, held.at[:, 0, 0:3]), "g2f": (2,),
        "g3": (3, held.at[:, 0:3]), "g3r": (3,), "g3f": (3,),
        "products": (4, acc),
        "s1": (5, grads.at[:, 0:3]), "s2": (5,), "s2u": (5,), "s3": (6, grads.at[:, 0, 0:3]), "s4": (6,),
        "s5": (7, grads.at[:, 0, 0, 0:3]), "s6": (7,),
        "end": (8, finals.at[0:3]),
    }

    def coming(key):
        name, p = key[0], key[1]
        if name in ("rows", "end"):
            return (name,), stage.at[2] if name == "rows" else finals.at[0:3]
        if name == "products":
            return key, other.at[0:384]
        if name == "g3f":
            return (name, key[3]), held.at[:, 0, 0]
        ref = held if name[0] == "g" else grads
        if name in ("g1", "s6"):
            return (name, p), ref.at[p, 0, 0, 0:2]
        if name in ("g1f", "s5"):
            return (name, p), ref.at[p, 0, 0, 0]
        if name in ("g2f", "s3"):
            return (name, p), ref.at[p, 0, 0]
        if name == "g3":
            return (name, p), ref.at[p, 0, 0:2]
        if name in ("g2", "s2u", "s4"):
            return (name, p, key[3]), ref.at[p, 0, 0, 0:2]
        if name == "s1":
            return (name, p, key[3]), ref.at[p, 0, 0]
        return (name, p, key[3]), ref.at[p, 0, 0:2]

    def send(key, source, target, to):
        group = coming(key)[0]
        index = groups.setdefault(group, len(groups))
        pltpu.make_async_remote_copy(
            src_ref=source,
            dst_ref=target,
            send_sem=send_sems.at[leaving[key[0]][0]],
            recv_sem=recv_sems.at[index],
            device_id=to,
            device_id_type=MESH,
        ).start()

    def arrived(*keys):
        for key in keys:
            group, view = coming(key)
            if group not in seen:
                seen.add(group)
                pltpu.make_async_copy(view, view, recv_sems.at[groups[group]]).wait()

    for copy in old:
        copy.wait()

    def fresh(columns):
        return adam_update(
            old_params[:, columns], old_moment[:, columns], old_second[:, columns], old_grad[:, columns]
        )[0]

    stage[0] = fresh(slice(0, 256))
    stage[1] = fresh(slice(256, 512))

    pl.semaphore_wait(barrier, len(greeted))

    send(("rows", 0), stage.at[1 - core], stage.at[2], sibling)

    def load_sibling(source):
        return pltpu.make_async_remote_copy(
            src_ref=source,
            dst_ref=act.at[mine],
            send_sem=local_sems.at[1],
            recv_sem=local_sems.at[2],
            device_id=sibling,
            device_id_type=MESH,
        )

    @pl.when(core == 0)
    def _():
        load_sibling(cotangent).start()

    @pl.when(core == 1)
    def _():
        load_sibling(tokens).start()

    def places(p):
        return tuple(own[axis] for axis in ORDER[p])

    arrived(("rows", 0))
    for first_core in range(2):
        @pl.when(core == first_core)
        def _():
            low, high = (stage[first_core], stage[2]) if first_core == 0 else (stage[2], stage[first_core])
            pieces = (low[:64], jnp.concatenate([low[64:], high[:32]], axis=0), high[32:])
            for p in range(3):
                one, two, three = places(p)
                held[p, three, two, one] = pieces[p]

    def half(way, rows):
        return pl.ds(SIDE[way] * (rows // 2), rows // 2)

    def unit(p, three, two, one):
        return held.at[p, three, two, one]

    def give(key, p, level, ref):
        for way in WAYS:
            send((key[0], p, way) + key[1:], ref, ref, neighbours[ORDER[p][level], way])

    def pass_on(key, p, level, way, ref):
        send(key, ref, ref, neighbours[ORDER[p][level], way])

    def give_own(p, level):
        one, two, three = places(p)
        give((f"g{level + 1}",) + ((0,) if level else ()), p, level, unit(p, three, two, one))

    def pass_first(p):
        one, two, three = places(p)
        for way in WAYS:
            arrived(("g1", p, way))
            pass_on(("g1f", p, way), p, 0, way, held.at[p, three, two, ring(one, -way), half(way, 64)])

    def give_unit(p, level, step):
        one, two, three = places(p)
        arrived(("g1f" if step == 2 else "g1", p, 1))
        give((f"g{level + 1}", step), p, level, unit(p, three, two, ring(one, step)))

    def pass_second(p, step):
        one, two, three = places(p)
        for way in WAYS:
            arrived(("g2", p, way, step))
            pass_on(
                ("g2f", p, way, step), p, 1, way,
                held.at[p, three, ring(two, -way), ring(one, step), half(way, 64)],
            )

    def give_row(p, step):
        one, two, three = places(p)
        if step == 2:
            arrived(*[("g2f", p, way, k) for way in WAYS for k in STEPS])
        else:
            arrived(*[("g2", p, -step, k) for k in STEPS])
        give(("g3r", step), p, 2, held.at[p, three, ring(two, step)])

    def third(p, way, step):
        return [("g3", p, way, k) for k in STEPS] if step == 0 else [("g3r", p, way, step)]

    def pass_third(p, step):
        one, two, three = places(p)
        for way in WAYS:
            arrived(*third(p, way, step))
            pass_on(
                ("g3f", p, way, step), p, 2, way,
                held.at[p, ring(three, -way), ring(two, step), :, half(way, 64)],
            )

    def block(p, x, y, z):
        place = (x, y, z)
        return tuple(place[axis] for axis in reversed(ORDER[p]))

    def columns(x, part, z):
        return pl.ds(pl.multiple_of(x * 3072 + part * 1536 + z * 384, 128), 384)

    def chunk_product(chunks, rows=slice(None)):
        left, right = [], []
        for step_x, flip, step_z in chunks:
            x, part, z = ring(own[0], step_x), lax.rem(y_hi + flip, 2), ring(own[2], step_z)
            left.append(act[rows, columns(x, part, z)])
            right += [held[(p,) + block(p, x, part * 2 + low, z)] for low in range(2) for p in range(3)]
        return jnp.dot(
            jnp.concatenate(left, axis=1), jnp.concatenate(right, axis=0), preferred_element_type=f32
        )

    near = (0, 1, -1)

    def multiply(which):
        if "loaded" not in seen:
            seen.add("loaded")
            load_own(tokens).wait()
            load_sibling(tokens).wait()
        for p in range(3):
            arrived(("g1", p, 1), ("g1f", p, 1), *[("g2", p, 1, k) for k in STEPS])
            if which >= 3:
                arrived(("g2f", p, 1, 0))
            for way in WAYS:
                for step in near:
                    arrived(*third(p, way, step))
                if which >= 3:
                    arrived(*third(p, way, 2))
                    for step in near[: which - 2]:
                        arrived(("g3f", p, way, step))
        if which < 3:
            todo = [(near[which], 0, z) for z in near]
        elif which < 6:
            todo = [(near[which - 3], 1, z) for z in near]
        elif which == 6:
            todo = [(2, 0, z) for z in near]
        else:
            todo = [(x, 0, 2) for x in near]
        part = chunk_product(todo)
        if which:
            acc[...] += part
        else:
            acc[...] = part

    actions = {
        "own": give_own, "first": pass_first, "unit": give_unit, "second": pass_second,
        "row": give_row, "third": pass_third, "mul": multiply,
    }
    for name, *rest in GATHER:
        actions[name](*rest)
    for p in range(3):
        for way in WAYS:
            arrived(("g3f", p, way, 2))
    last = [(2, 0, 2)] + [(2, 1, z) for z in (0, 1, -1, 2)] + [(x, 1, 2) for x in near]
    for index in range(2):
        rows = slice(index * 384, index * 384 + 384)
        acc[rows] += chunk_product(last, rows)
        send(("products", index), acc.at[rows], other.at[rows], sibling)
    for index in range(2):
        arrived(("products", index))
        for start in range(index * 384, index * 384 + 384, 128):
            span = slice(start, start + 128)

            @pl.when(core == 0)
            def _():
                turned[:, span] = (other[span] * gelu_slope(acc[span])).T.astype(bf16)

            @pl.when(core == 1)
            def _():
                turned[:, span] = gelu_value(other[span]).T.astype(bf16)

    def term(x, z):
        right = jnp.concatenate([act[:, columns(x, part, z)] for part in range(2)], axis=1)
        result = jnp.dot(turned[...], right, preferred_element_type=f32).astype(bf16)
        for part in range(2):
            for p in range(3):
                for low in range(2):
                    start = (part * 3 + p) * 128
                    grads[(p,) + block(p, x, part * 2 + low, z)] = result[
                        low * 128 : low * 128 + 128, start : start + 128
                    ]

    def terms(which):
        x, z = own[0], own[2]
        if which == 0:
            term(ring(x, 2), ring(z, 2))
        else:
            def body(step, carry):
                off = step - 1
                if which == 1:
                    term(ring(x, 2), ring(z, off))
                elif which == 2:
                    term(ring(x, off), ring(z, 2))
                else:
                    term(ring(x, (1, -1, 0)[which - 3]), ring(z, off))
                return carry

            lax.fori_loop(0, 3, body, 0)

    def send_first(p, step):
        one, two, three = places(p)
        for way in WAYS:
            send(
                ("s1", p, way, step),
                grads.at[p, ring(three, 2), ring(two, step), :, half(way, 128)],
                first_rows.at[p, SIDE[way], SLOT[step]],
                neighbours[ORDER[p][2], way],
            )

    def add_first(p, way, step):
        one, two, three = places(p)
        arrived(("s1", p, way, step))
        ref = grads.at[p, ring(three, way), ring(two, step), :, half(way, 128)]
        ref[...] = (ref[...].astype(f32) + first_rows[p, SIDE[way], SLOT[step]].astype(f32)).astype(bf16)

    def send_row(p, step):
        one, two, three = places(p)
        for way in WAYS:
            add_first(p, way, step)
            send(
                ("s2", p, way, step),
                grads.at[p, ring(three, way), ring(two, step)],
                full_rows.at[p, SIDE[way], SLOT[step]],
                neighbours[ORDER[p][2], way],
            )

    def send_own_row(p, step):
        one, two, three = places(p)
        for way in WAYS:
            if ("added", p, way) not in seen:
                seen.add(("added", p, way))
                add_first(p, way, 0)
            send(
                ("s2u", p, way, step),
                grads.at[p, ring(three, way), two, ring(one, step)],
                full_units.at[p, SIDE[way], SLOT[step]],
                neighbours[ORDER[p][2], way],
            )

    def sum_row(p, step):
        one, two, three = places(p)
        arrived(*[("s2", p, way, step) for way in WAYS])
        return (
            grads[p, three, ring(two, step)].astype(f32)
            + full_rows[p, 0, SLOT[step]].astype(f32)
            + full_rows[p, 1, SLOT[step]].astype(f32)
        )

    def send_second(p):
        one, two, three = places(p)
        grads[p, three, ring(two, 2)] = sum_row(p, 2).astype(bf16)
        for way in WAYS:
            send(
                ("s3", p, way),
                grads.at[p, three, ring(two, 2), :, half(way, 128)],
                first_second.at[p, SIDE[way]],
                neighbours[ORDER[p][1], way],
            )

    def add_second(p):
        one, two, three = places(p)
        for way in WAYS:
            row = sum_row(p, way)
            arrived(("s3", p, way))
            low, high = row[:, :64], row[:, 64:]
            extra = first_second[p, SIDE[way]].astype(f32)
            low, high = (low + extra, high) if way == 1 else (low, high + extra)
            grads[p, three, ring(two, way), :, :64] = low.astype(bf16)
            grads[p, three, ring(two, way), :, 64:] = high.astype(bf16)

    def send_unit(p, step):
        one, two, three = places(p)
        for way in WAYS:
            send(
                ("s4", p, way, step),
                grads.at[p, three, ring(two, way), ring(one, step)],
                second_units.at[p, SIDE[way], SLOT[step]],
                neighbours[ORDER[p][1], way],
            )

    def sum_unit(p, step):
        one, two, three = places(p)
        total = grads[p, three, two, ring(one, step)].astype(f32)
        for way in WAYS:
            arrived(("s2u", p, way, step))
            total += full_units[p, SIDE[way], SLOT[step]].astype(f32)
        for way in WAYS:
            arrived(("s4", p, way, step))
            total += second_units[p, SIDE[way], SLOT[step]].astype(f32)
        return total

    def send_third(p):
        one, two, three = places(p)
        grads[p, three, two, ring(one, 2)] = sum_unit(p, 2).astype(bf16)
        for way in WAYS:
            send(
                ("s5", p, way),
                grads.at[p, three, two, ring(one, 2), half(way, 128)],
                first_last.at[p, SIDE[way]],
                neighbours[ORDER[p][0], way],
            )

    def send_last(p):
        one, two, three = places(p)
        for way in WAYS:
            total = sum_unit(p, way)
            arrived(("s5", p, way))
            low, high = total[:64], total[64:]
            extra = first_last[p, SIDE[way]].astype(f32)
            low, high = (low + extra, high) if way == 1 else (low, high + extra)
            grads[p, three, two, ring(one, way), :64] = low.astype(bf16)
            grads[p, three, two, ring(one, way), 64:] = high.astype(bf16)
            send(
                ("s6", p, way),
                grads.at[p, three, two, ring(one, way)],
                last_unit.at[p, SIDE[way]],
                neighbours[ORDER[p][0], way],
            )

    def finish(p):
        total = sum_unit(p, 0)
        for way in WAYS:
            arrived(("s6", p, way))
            total += last_unit[p, SIDE[way]].astype(f32)
        final[p * 128 : p * 128 + 128] = total.T

    actions = {
        "terms": terms, "first": send_first, "row": send_row, "own": send_own_row, "second": send_second,
        "add": add_second, "unit": send_unit, "third": send_third, "last": send_last, "end": finish,
    }
    for name, *rest in SCATTER:
        actions[name](*rest)

    index = y_lo * 2 + core
    for which in (3, 2, 1):
        to = lax.rem(y_lo + which // 2, 2) * 2 + lax.rem(core + which % 2, 2)
        send(
            ("end", which),
            final.at[pl.ds(pl.multiple_of(to * 96, 96), 96)],
            finals.at[index],
            partner(which),
        )
    finals[index] = final[pl.ds(pl.multiple_of(index * 96, 96), 96)]
    for which in (1, 2, 3):
        arrived(("end", which))
    for source in range(4):
        start = (source % 2) * 256 + (source // 2) * 128
        gradient_out[0, :, start : start + 128] = finals[source]

    for index, *view in leaving.values():
        if view:
            pltpu.make_async_copy(view[0], view[0], send_sems.at[index]).wait()


def per_device(params, moment, second, grad_prev, tokens, cotangent):
    shard = (1, 96, 512)
    gradient = pl.pallas_call(
        kernel,
        out_shape=jax.ShapeDtypeStruct(shard, f32),
        in_specs=[pl.BlockSpec(memory_space=pl.ANY)] * 6,
        out_specs=pl.BlockSpec(memory_space=pltpu.VMEM),
        scratch_shapes=[
            pltpu.VMEM((768, 12288), bf16),
            pltpu.VMEM((3, 4, 4, 4, 64, 256), bf16),
            pltpu.VMEM((3, 4, 4, 4, 128, 128), bf16),
            pltpu.VMEM((768, 256), f32),
            pltpu.VMEM((768, 256), f32),
            pltpu.VMEM((256, 768), bf16),
            pltpu.VMEM((3, 96, 256), bf16),
            pltpu.VMEM((96, 512), bf16),
            pltpu.VMEM((96, 512), bf16),
            pltpu.VMEM((96, 512), bf16),
            pltpu.VMEM((96, 512), f32),
            pltpu.VMEM((3, 2, 4, 4, 64, 128), bf16),
            pltpu.VMEM((3, 2, 3, 4, 128, 128), bf16),
            pltpu.VMEM((3, 2, 4, 128, 128), bf16),
            pltpu.VMEM((3, 2, 4, 64, 128), bf16),
            pltpu.VMEM((3, 2, 4, 128, 128), bf16),
            pltpu.VMEM((3, 2, 64, 128), bf16),
            pltpu.VMEM((3, 2, 128, 128), bf16),
            pltpu.VMEM((384, 128), f32),
            pltpu.VMEM((4, 96, 128), f32),
            pltpu.SemaphoreType.DMA((9,)),
            pltpu.SemaphoreType.DMA((95,)),
            pltpu.SemaphoreType.DMA((7,)),
        ],
        compiler_params=pltpu.CompilerParams(
            collective_id=0, has_side_effects=True, vmem_limit_bytes=56 * 2**20
        ),
    )(params, moment, second, grad_prev, tokens, cotangent)
    return adam_update(params, moment, second, grad_prev) + (gradient,)


def solution(mesh):
    blocks = P("inner", "outer", None)
    rows = P(("outer", "inner"), None)
    return jax.shard_map(
        per_device,
        mesh=mesh,
        in_specs=(blocks,) * 4 + (rows,) * 2,
        out_specs=(blocks,) * 4,
        check_vma=False,
    )
```

time: 102 us -> 86 us (0.84)
  Pallas kernels: 94.1 us -> 82.6 us
  local copies, waits for them, and re-layouts: 6.23 us -> 1.63 us
    pallas_call x1, Pallas kernels: 94.1 us -> 82.6 us  [per_device(): pl.pallas_call(kernel, out_shape=jax.ShapeDtypeStruct(shard, f32), in_spe...]
    unnamed x4 -> x9, local copies, waits for them, and re-layouts: 6.23 us -> 1.63 us
where the time goes in v2:
time: 86 us; the launch traced here: 85.9 us
  Pallas kernels  82.6 us (96%)
  local copies, waits for them, and re-layouts  1.63 us (2%)
  other arithmetic  0.93 us (1%)
    pallas_call x1, Pallas kernels, per_device(): pl.pallas_call(kernel, out_shape=jax.ShapeDtypeStruct(shard, f32), in_spe...  82.6 us

profile of v2, /device:TPU:1, one launch (start us, length us, event | category | flops | bytes accessed | tf_op | source)
XLA Modules:
  0.0 85.9 jit_solution(9244710123229391419)
XLA Ops:
  0.6 0.0 copy-start
  0.6 0.0 copy-start.1
  0.7 0.0 copy-start.2
  0.7 0.0 copy-start.3
  0.7 82.6 %shard_map.93 = f32[1,96,512]{2,1,0:T(8,128)} custom-call(bf16[1,96,512]{2,1,0:T(8,128)(2,1)} %params.1, bf16[1,96,512]{2,1,0:T(8,128)(2,1)} %moment.1, bf16[1,96,512]{2,1,0:T(8,128)(2,1)} %second.1, f32[1,96,512]{2,1,0:T(8,128)} %grad_prev.1, bf16[384,12288]{1,0:T(8,128)(2,1)} %tokens.1, bf16[384,12288]{1,0:T(8,128)(2,1)} %cotangent.1), custom_call_target="tpu_custom_call" | custom-call | tf_op jit(solution)/shard_map/pallas_call | solution.py:572
  83.3 0.0 copy-done
  83.3 0.0 copy-done.1
  83.3 0.0 copy-done.2
  83.3 0.0 copy-done.3
  83.3 0.9 %fusion.5 = (bf16[1,96,512]{2,1,0:T(8,128)(2,1)}, bf16[1,96,512]{2,1,0:T(8,128)(2,1)}, bf16[1,96,512]{2,1,0:T(8,128)(2,1)}) fusion(f32[1,96,512]{2,1,0:T(8,128)S(1)} %copy-done, bf16[1,96,512]{2,1,0:T(8,128)(2,1)S(1)} %copy-done.1, bf16[1,96,512]{2,1,0:T(8,128)(2,1)S(1)} %copy-done.2, bf16[1,96,512]{2,1,0:T(8,128)(2,1)S(1)} %copy-done.3), kind=kLoop, calls=%fused_computation.9 | loop fusion | flops 1032192 | bytes 786432 | tf_op jit(solution)/shard_map/convert_element_type | solution.py:50
  84.2 1.6 %copy.11 = f32[1,96,512]{2,1,0:T(8,128)} copy(f32[1,96,512]{2,1,0:T(8,128)} %shard_map.93) | data formatting | bytes 393216
Async XLA Ops:
  0.6 82.6 %copy-start = (f32[1,96,512]{2,1,0:T(8,128)S(1)}, f32[1,96,512]{2,1,0:T(8,128)}, u32[]{:S(2)}) copy-start(f32[1,96,512]{2,1,0:T(8,128)} %grad_prev.1) | copy-start | bytes 589828
  0.6 82.6 %copy-start.1 = (bf16[1,96,512]{2,1,0:T(8,128)(2,1)S(1)}, bf16[1,96,512]{2,1,0:T(8,128)(2,1)}, u32[]{:S(2)}) copy-start(bf16[1,96,512]{2,1,0:T(8,128)(2,1)} %second.1) | copy-start | bytes 294916
  0.7 82.6 %copy-start.2 = (bf16[1,96,512]{2,1,0:T(8,128)(2,1)S(1)}, bf16[1,96,512]{2,1,0:T(8,128)(2,1)}, u32[]{:S(2)}) copy-start(bf16[1,96,512]{2,1,0:T(8,128)(2,1)} %moment.1) | copy-start | bytes 294916
  0.7 82.6 %copy-start.3 = (bf16[1,96,512]{2,1,0:T(8,128)(2,1)S(1)}, bf16[1,96,512]{2,1,0:T(8,128)(2,1)}, u32[]{:S(2)}) copy-start(bf16[1,96,512]{2,1,0:T(8,128)(2,1)} %params.1) | copy-start | bytes 294916

commit v3 on v2

--- a/solution.py
+++ b/solution.py
@@ -59,47 +59,36 @@
 
 
 GATHER = (
-    *(("own", p, level) for level in range(3) for p in range(3)),
-    *(step for p in range(3) for step in (("first", p), ("unit", p, 1, 1), ("unit", p, 1, -1))),
-    *(("second", p, 0) for p in range(3)),
-    *(("unit", p, 2, step) for p in range(3) for step in (1, -1)),
-    *(("unit", p, 1, 2) for p in range(3)),
-    *(("unit", p, 2, 2) for p in range(3)),
-    *(("second", p, step) for p in range(3) for step in (1, -1)),
-    *(("second", p, 2) for p in range(3)),
-    *(("row", p, 1) for p in range(3)),
-    *(("third", p, 0) for p in range(3)),
-    *(("row", p, step) for p in range(3) for step in (2,)),
-    *(("row", p, -1) for p in range(3)),
-    *(("third", p, 1) for p in range(3)),
-    *(("third", p, -1) for p in range(3)),
-    ("mul", 0), ("mul", 1), ("mul", 2),
-    *(("third", p, 2) for p in range(3)),
-    ("mul", 3), ("mul", 4), ("mul", 5), ("mul", 6), ("mul", 7),
+    ("own", 1, 0), ("own", 0, 0), ("own", 2, 0), ("own", 2, 2), ("own", 0, 2), ("own", 1, 1), ("own", 2, 1),
+    ("own", 1, 2), ("own", 0, 1), ("first", 1), ("first", 0), ("first", 2), ("unit", 0, 1, -1), ("unit", 1, 1, -1),
+    ("unit", 0, 1, 1), ("unit", 2, 1, 1), ("unit", 2, 2, -1), ("unit", 2, 1, -1), ("unit", 0, 2, 1),
+    ("unit", 1, 2, 1), ("second", 2, 0), ("unit", 1, 1, 1), ("unit", 1, 1, 2), ("unit", 0, 1, 2), ("unit", 2, 2, 1),
+    ("unit", 2, 1, 2), ("unit", 0, 2, 2), ("unit", 2, 2, 2), ("second", 0, -1), ("unit", 1, 2, -1), ("second", 0, 0),
+    ("second", 1, -1), ("unit", 0, 2, -1), ("second", 0, 1), ("second", 1, 0), ("second", 2, 1), ("second", 2, -1),
+    ("second", 1, 1), ("unit", 1, 2, 2), ("second", 1, 2), ("row", 1, -1), ("second", 0, 2), ("row", 0, -1),
+    ("row", 2, -1), ("row", 2, 1), ("row", 0, 1), ("second", 2, 2), ("row", 1, 1), ("third", 1, 0), ("row", 1, 2),
+    ("row", 2, 2), ("row", 0, 2), ("third", 2, 0), ("third", 0, 0), ("mul", 0), ("third", 1, 1), ("third", 2, 1),
+    ("third", 0, 1), ("mul", 2), ("third", 0, -1), ("third", 1, -1), ("third", 2, -1), ("mul", 1), ("mul", 3),
+    ("third", 0, 2), ("third", 2, 2), ("third", 1, 2), ("mul", 4), ("mul", 5), ("mul", 6), ("mul", 7),
 )
 SCATTER = (
-    ("terms", 0), ("first", 1, 2),
-    ("terms", 1), ("first", 1, 1), ("first", 2, 2), ("first", 1, -1), ("first", 1, 0),
-    ("terms", 2), ("first", 0, 2), ("first", 0, 1), ("first", 0, -1), ("first", 0, 0),
-    ("terms", 3), ("first", 2, 1), ("terms", 4), ("first", 2, -1), ("terms", 5), ("first", 2, 0),
-    *(("row", p, 2) for p in range(3)),
-    *(("row", p, 1) for p in range(3)),
-    *(step for p in range(3) for step in (("row", p, -1), ("second", p))),
-    *(("own", p, 2) for p in range(3)),
-    *(step for p in range(3) for step in (("add", p), ("unit", p, 2), ("unit", p, 1), ("unit", p, -1))),
-    *(("own", p, step) for step in (1, -1) for p in range(3)),
-    *(("third", p) for p in range(3)),
-    *(("own", p, 0) for p in range(3)),
-    *(("unit", p, 0) for p in range(3)),
-    *(("last", p) for p in range(3)),
-    *(("end", p) for p in range(3)),
+    ("terms", 0), ("first", 1, 2), ("terms", 1), ("first", 1, 1), ("first", 2, 2), ("first", 1, -1), ("first", 1, 0),
+    ("terms", 2), ("first", 0, 2), ("first", 0, 1), ("first", 0, -1), ("first", 0, 0), ("terms", 3), ("first", 2, 1),
+    ("terms", 4), ("first", 2, -1), ("terms", 5), ("first", 2, 0), ("row", 0, 2), ("row", 1, 2), ("row", 2, 2),
+    ("row", 0, 1), ("row", 1, 1), ("row", 2, 1), ("row", 0, -1), ("second", 0), ("row", 1, -1), ("second", 1),
+    ("row", 2, -1), ("second", 2), ("own", 0, 2), ("own", 1, 2), ("own", 2, 2), ("add", 0), ("unit", 0, 2),
+    ("unit", 0, 1), ("unit", 0, -1), ("add", 1), ("unit", 1, 2), ("unit", 1, 1), ("unit", 1, -1), ("add", 2),
+    ("unit", 2, 2), ("unit", 2, 1), ("unit", 2, -1), ("own", 0, 1), ("own", 1, 1), ("own", 2, 1), ("own", 0, -1),
+    ("own", 1, -1), ("own", 2, -1), ("third", 0), ("third", 1), ("third", 2), ("own", 0, 0), ("own", 1, 0),
+    ("own", 2, 0), ("unit", 0, 0), ("unit", 1, 0), ("unit", 2, 0), ("last", 0), ("last", 1), ("last", 2), ("end", 0),
+    ("end", 1), ("end", 2),
 )
 
 
 def kernel(
     params, moment, second, grad_prev, tokens, cotangent,
     gradient_out,
-    act, held, grads, acc, other, turned, stage,
+    act, held, grads, acc, other, factor, stage,
     old_params, old_moment, old_second, old_grad,
     first_rows, full_rows, full_units, first_second, second_units, first_last, last_unit,
     final, finals, send_sems, recv_sems, local_sems,
@@ -116,16 +105,11 @@
         place[axis] = ring(place[axis], way)
         return device(*place, core)
 
-    def partner(which):
-        return device(
-            own[0], own[1] - y_lo + lax.rem(y_lo + which // 2, 2), own[2], lax.rem(core + which % 2, 2)
-        )
-
     neighbours = {(axis, way): neighbour(axis, way) for axis in range(3) for way in WAYS}
-    sibling = partner(1)
+    sibling = device(*own, 1 - core)
 
     barrier = pltpu.get_barrier_semaphore()
-    greeted = list(neighbours.values()) + [sibling, partner(3)]
+    greeted = list(neighbours.values()) + [sibling]
     for one in greeted:
         pl.semaphore_signal(barrier, inc=1, device_id=one, device_id_type=MESH)
 
@@ -160,13 +144,13 @@
         "products": (4, acc),
         "s1": (5, grads.at[:, 0:3]), "s2": (5,), "s2u": (5,), "s3": (6, grads.at[:, 0, 0:3]), "s4": (6,),
         "s5": (7, grads.at[:, 0, 0, 0:3]), "s6": (7,),
-        "end": (8, finals.at[0:3]),
+        "end": (8, finals),
     }
 
     def coming(key):
         name, p = key[0], key[1]
         if name in ("rows", "end"):
-            return (name,), stage.at[2] if name == "rows" else finals.at[0:3]
+            return (name,), stage.at[2] if name == "rows" else finals
         if name == "products":
             return key, other.at[0:384]
         if name == "g3f":
@@ -378,46 +362,46 @@
 
             @pl.when(core == 0)
             def _():
-                turned[:, span] = (other[span] * gelu_slope(acc[span])).T.astype(bf16)
+                factor[span] = (other[span] * gelu_slope(acc[span])).astype(bf16)
 
             @pl.when(core == 1)
             def _():
-                turned[:, span] = gelu_value(other[span]).T.astype(bf16)
+                factor[span] = gelu_value(other[span]).astype(bf16)
 
     def term(x, z):
-        right = jnp.concatenate([act[:, columns(x, part, z)] for part in range(2)], axis=1)
-        result = jnp.dot(turned[...], right, preferred_element_type=f32).astype(bf16)
         for part in range(2):
-            for p in range(3):
-                for low in range(2):
-                    start = (part * 3 + p) * 128
-                    grads[(p,) + block(p, x, part * 2 + low, z)] = result[
-                        low * 128 : low * 128 + 128, start : start + 128
-                    ]
+            result = lax.dot_general(
+                act[:, columns(x, part, z)], factor[...], (((0,), (0,)), ((), ())), preferred_element_type=f32
+            ).astype(bf16)
+            for low in range(2):
+                for p in range(3):
+                    start = (low * 3 + p) * 64
+                    grads[(p,) + block(p, x, part * 2 + low, z)] = result[start : start + 64]
 
     def terms(which):
         x, z = own[0], own[2]
         if which == 0:
             term(ring(x, 2), ring(z, 2))
-        else:
-            def body(step, carry):
-                off = step - 1
-                if which == 1:
-                    term(ring(x, 2), ring(z, off))
-                elif which == 2:
-                    term(ring(x, off), ring(z, 2))
-                else:
-                    term(ring(x, (1, -1, 0)[which - 3]), ring(z, off))
-                return carry
-
-            lax.fori_loop(0, 3, body, 0)
+            return
+
+        def body(index, carry):
+            step = index - 1
+            if which < 2:
+                term(ring(x, 2), ring(z, step))
+            elif which == 2:
+                term(ring(x, step), ring(z, 2))
+            else:
+                term(ring(x, (1, -1, 0)[which - 3]), ring(z, step))
+            return carry
+
+        lax.fori_loop(0, 3, body, 0)
 
     def send_first(p, step):
         one, two, three = places(p)
         for way in WAYS:
             send(
                 ("s1", p, way, step),
-                grads.at[p, ring(three, 2), ring(two, step), :, half(way, 128)],
+                grads.at[p, ring(three, 2), ring(two, step), :, half(way, 64)],
                 first_rows.at[p, SIDE[way], SLOT[step]],
                 neighbours[ORDER[p][2], way],
             )
@@ -425,7 +409,7 @@
     def add_first(p, way, step):
         one, two, three = places(p)
         arrived(("s1", p, way, step))
-        ref = grads.at[p, ring(three, way), ring(two, step), :, half(way, 128)]
+        ref = grads.at[p, ring(three, way), ring(two, step), :, half(way, 64)]
         ref[...] = (ref[...].astype(f32) + first_rows[p, SIDE[way], SLOT[step]].astype(f32)).astype(bf16)
 
     def send_row(p, step):
@@ -467,7 +451,7 @@
         for way in WAYS:
             send(
                 ("s3", p, way),
-                grads.at[p, three, ring(two, 2), :, half(way, 128)],
+                grads.at[p, three, ring(two, 2), :, half(way, 64)],
                 first_second.at[p, SIDE[way]],
                 neighbours[ORDER[p][1], way],
             )
@@ -477,11 +461,11 @@
         for way in WAYS:
             row = sum_row(p, way)
             arrived(("s3", p, way))
-            low, high = row[:, :64], row[:, 64:]
+            low, high = row[:, :32], row[:, 32:]
             extra = first_second[p, SIDE[way]].astype(f32)
             low, high = (low + extra, high) if way == 1 else (low, high + extra)
-            grads[p, three, ring(two, way), :, :64] = low.astype(bf16)
-            grads[p, three, ring(two, way), :, 64:] = high.astype(bf16)
+            grads[p, three, ring(two, way), :, :32] = low.astype(bf16)
+            grads[p, three, ring(two, way), :, 32:] = high.astype(bf16)
 
     def send_unit(p, step):
         one, two, three = places(p)
@@ -510,7 +494,7 @@
         for way in WAYS:
             send(
                 ("s5", p, way),
-                grads.at[p, three, two, ring(one, 2), half(way, 128)],
+                grads.at[p, three, two, ring(one, 2), half(way, 64)],
                 first_last.at[p, SIDE[way]],
                 neighbours[ORDER[p][0], way],
             )
@@ -520,11 +504,11 @@
         for way in WAYS:
             total = sum_unit(p, way)
             arrived(("s5", p, way))
-            low, high = total[:64], total[64:]
+            low, high = total[:32], total[32:]
             extra = first_last[p, SIDE[way]].astype(f32)
             low, high = (low + extra, high) if way == 1 else (low, high + extra)
-            grads[p, three, two, ring(one, way), :64] = low.astype(bf16)
-            grads[p, three, two, ring(one, way), 64:] = high.astype(bf16)
+            grads[p, three, two, ring(one, way), :32] = low.astype(bf16)
+            grads[p, three, two, ring(one, way), 32:] = high.astype(bf16)
             send(
                 ("s6", p, way),
                 grads.at[p, three, two, ring(one, way)],
@@ -537,7 +521,7 @@
         for way in WAYS:
             arrived(("s6", p, way))
             total += last_unit[p, SIDE[way]].astype(f32)
-        final[p * 128 : p * 128 + 128] = total.T
+        final[p * 64 : p * 64 + 64] = total
 
     actions = {
         "terms": terms, "first": send_first, "row": send_row, "own": send_own_row, "second": send_second,
@@ -546,21 +530,14 @@
     for name, *rest in SCATTER:
         actions[name](*rest)
 
-    index = y_lo * 2 + core
-    for which in (3, 2, 1):
-        to = lax.rem(y_lo + which // 2, 2) * 2 + lax.rem(core + which % 2, 2)
-        send(
-            ("end", which),
-            final.at[pl.ds(pl.multiple_of(to * 96, 96), 96)],
-            finals.at[index],
-            partner(which),
-        )
-    finals[index] = final[pl.ds(pl.multiple_of(index * 96, 96), 96)]
-    for which in (1, 2, 3):
-        arrived(("end", which))
-    for source in range(4):
-        start = (source % 2) * 256 + (source // 2) * 128
-        gradient_out[0, :, start : start + 128] = finals[source]
+    def rows_of(which):
+        return pl.ds(pl.multiple_of(which * 96, 96), 96)
+
+    send(("end", 0), final.at[rows_of(1 - core)], finals, sibling)
+    mine_sum = final[rows_of(core)]
+    arrived(("end", 0))
+    gradient_out[0, :, :256] = jnp.where(core == 0, mine_sum, finals[...])
+    gradient_out[0, :, 256:] = jnp.where(core == 0, finals[...], mine_sum)
 
     for index, *view in leaving.values():
         if view:
@@ -571,30 +548,30 @@
     shard = (1, 96, 512)
     gradient = pl.pallas_call(
         kernel,
-        out_shape=jax.ShapeDtypeStruct(shard, f32),
+        out_shape=pltpu.VMEM(shard, f32),
         in_specs=[pl.BlockSpec(memory_space=pl.ANY)] * 6,
         out_specs=pl.BlockSpec(memory_space=pltpu.VMEM),
         scratch_shapes=[
             pltpu.VMEM((768, 12288), bf16),
             pltpu.VMEM((3, 4, 4, 4, 64, 256), bf16),
-            pltpu.VMEM((3, 4, 4, 4, 128, 128), bf16),
+            pltpu.VMEM((3, 4, 4, 4, 64, 256), bf16),
             pltpu.VMEM((768, 256), f32),
             pltpu.VMEM((768, 256), f32),
-            pltpu.VMEM((256, 768), bf16),
+            pltpu.VMEM((768, 256), bf16),
             pltpu.VMEM((3, 96, 256), bf16),
             pltpu.VMEM((96, 512), bf16),
             pltpu.VMEM((96, 512), bf16),
             pltpu.VMEM((96, 512), bf16),
             pltpu.VMEM((96, 512), f32),
-            pltpu.VMEM((3, 2, 4, 4, 64, 128), bf16),
-            pltpu.VMEM((3, 2, 3, 4, 128, 128), bf16),
-            pltpu.VMEM((3, 2, 4, 128, 128), bf16),
-            pltpu.VMEM((3, 2, 4, 64, 128), bf16),
-            pltpu.VMEM((3, 2, 4, 128, 128), bf16),
-            pltpu.VMEM((3, 2, 64, 128), bf16),
-            pltpu.VMEM((3, 2, 128, 128), bf16),
-            pltpu.VMEM((384, 128), f32),
-            pltpu.VMEM((4, 96, 128), f32),
+            pltpu.VMEM((3, 2, 4, 4, 32, 256), bf16),
+            pltpu.VMEM((3, 2, 3, 4, 64, 256), bf16),
+            pltpu.VMEM((3, 2, 4, 64, 256), bf16),
+            pltpu.VMEM((3, 2, 4, 32, 256), bf16),
+            pltpu.VMEM((3, 2, 4, 64, 256), bf16),
+            pltpu.VMEM((3, 2, 32, 256), bf16),
+            pltpu.VMEM((3, 2, 64, 256), bf16),
+            pltpu.VMEM((192, 256), f32),
+            pltpu.VMEM((96, 256), f32),
             pltpu.SemaphoreType.DMA((9,)),
             pltpu.SemaphoreType.DMA((95,)),
             pltpu.SemaphoreType.DMA((7,)),

time: 86 us -> 79.7 us (0.927)
  Pallas kernels: 82.6 us -> 77.3 us
  local copies, waits for them, and re-layouts: 1.63 us -> 0.7 us
    pallas_call x1, Pallas kernels: 82.6 us -> 77.3 us  [per_device(): pl.pallas_call(kernel, out_shape=pltpu.VMEM(shard, f32), in_specs=[pl.Blo...]
    unnamed x9, local copies, waits for them, and re-layouts: 1.63 us -> 0.7 us
where the time goes in v3:
time: 79.7 us; the launch traced here: 79.6 us
  Pallas kernels  77.3 us (97%)
  other arithmetic  0.93 us (1%)
    pallas_call x1, Pallas kernels, per_device(): pl.pallas_call(kernel, out_shape=pltpu.VMEM(shard, f32), in_specs=[pl.Blo...  77.3 us

profile of v3, /device:TPU:1, one launch (start us, length us, event | category | flops | bytes accessed | tf_op | source)
XLA Modules:
  0.0 79.6 jit_solution(7600632655607768567)
XLA Ops:
  0.6 0.0 copy-start
  0.6 0.0 copy-start.1
  0.7 0.0 copy-start.2
  0.7 0.0 copy-start.3
  0.7 77.3 %shard_map.93 = f32[1,96,512]{2,1,0:T(8,128)S(1)} custom-call(bf16[1,96,512]{2,1,0:T(8,128)(2,1)} %params.1, bf16[1,96,512]{2,1,0:T(8,128)(2,1)} %moment.1, bf16[1,96,512]{2,1,0:T(8,128)(2,1)} %second.1, f32[1,96,512]{2,1,0:T(8,128)} %grad_prev.1, bf16[384,12288]{1,0:T(8,128)(2,1)} %tokens.1, bf16[384,12288]{1,0:T(8,128)(2,1)} %cotangent.1), custom_call_target="tpu_custom_call" | custom-call | tf_op jit(solution)/shard_map/pallas_call | solution.py:549
  78.0 0.7 copy.11
  78.6 0.0 copy-done
  78.7 0.0 copy-done.1
  78.7 0.0 copy-done.2
  78.7 0.0 copy-done.3
  78.7 0.9 %fusion.5 = (bf16[1,96,512]{2,1,0:T(8,128)(2,1)}, bf16[1,96,512]{2,1,0:T(8,128)(2,1)}, bf16[1,96,512]{2,1,0:T(8,128)(2,1)}) fusion(f32[1,96,512]{2,1,0:T(8,128)S(1)} %copy-done, bf16[1,96,512]{2,1,0:T(8,128)(2,1)S(1)} %copy-done.1, bf16[1,96,512]{2,1,0:T(8,128)(2,1)S(1)} %copy-done.2, bf16[1,96,512]{2,1,0:T(8,128)(2,1)S(1)} %copy-done.3), kind=kLoop, calls=%fused_computation.9 | loop fusion | flops 1032192 | bytes 786432 | tf_op jit(solution)/shard_map/convert_element_type | solution.py:50
Async XLA Ops:
  0.6 78.0 %copy-start = (f32[1,96,512]{2,1,0:T(8,128)S(1)}, f32[1,96,512]{2,1,0:T(8,128)}, u32[]{:S(2)}) copy-start(f32[1,96,512]{2,1,0:T(8,128)} %grad_prev.1) | copy-start | bytes 589828
  0.6 78.0 %copy-start.1 = (bf16[1,96,512]{2,1,0:T(8,128)(2,1)S(1)}, bf16[1,96,512]{2,1,0:T(8,128)(2,1)}, u32[]{:S(2)}) copy-start(bf16[1,96,512]{2,1,0:T(8,128)(2,1)} %second.1) | copy-start | bytes 294916
  0.7 78.0 %copy-start.2 = (bf16[1,96,512]{2,1,0:T(8,128)(2,1)S(1)}, bf16[1,96,512]{2,1,0:T(8,128)(2,1)}, u32[]{:S(2)}) copy-start(bf16[1,96,512]{2,1,0:T(8,128)(2,1)} %moment.1) | copy-start | bytes 294916
  0.7 78.0 %copy-start.3 = (bf16[1,96,512]{2,1,0:T(8,128)(2,1)S(1)}, bf16[1,96,512]{2,1,0:T(8,128)(2,1)}, u32[]{:S(2)}) copy-start(bf16[1,96,512]{2,1,0:T(8,128)(2,1)} %params.1) | copy-start | bytes 294916

commit v4 on v3

--- a/solution.py
+++ b/solution.py
@@ -60,28 +60,27 @@
 
 GATHER = (
     ("own", 1, 0), ("own", 0, 0), ("own", 2, 0), ("own", 2, 2), ("own", 0, 2), ("own", 1, 1), ("own", 2, 1),
-    ("own", 1, 2), ("own", 0, 1), ("first", 1), ("first", 0), ("first", 2), ("unit", 0, 1, -1), ("unit", 1, 1, -1),
-    ("unit", 0, 1, 1), ("unit", 2, 1, 1), ("unit", 2, 2, -1), ("unit", 2, 1, -1), ("unit", 0, 2, 1),
-    ("unit", 1, 2, 1), ("second", 2, 0), ("unit", 1, 1, 1), ("unit", 1, 1, 2), ("unit", 0, 1, 2), ("unit", 2, 2, 1),
-    ("unit", 2, 1, 2), ("unit", 0, 2, 2), ("unit", 2, 2, 2), ("second", 0, -1), ("unit", 1, 2, -1), ("second", 0, 0),
-    ("second", 1, -1), ("unit", 0, 2, -1), ("second", 0, 1), ("second", 1, 0), ("second", 2, 1), ("second", 2, -1),
-    ("second", 1, 1), ("unit", 1, 2, 2), ("second", 1, 2), ("row", 1, -1), ("second", 0, 2), ("row", 0, -1),
-    ("row", 2, -1), ("row", 2, 1), ("row", 0, 1), ("second", 2, 2), ("row", 1, 1), ("third", 1, 0), ("row", 1, 2),
-    ("row", 2, 2), ("row", 0, 2), ("third", 2, 0), ("third", 0, 0), ("mul", 0), ("third", 1, 1), ("third", 2, 1),
-    ("third", 0, 1), ("mul", 2), ("third", 0, -1), ("third", 1, -1), ("third", 2, -1), ("mul", 1), ("mul", 3),
-    ("third", 0, 2), ("third", 2, 2), ("third", 1, 2), ("mul", 4), ("mul", 5), ("mul", 6), ("mul", 7),
+    ("own", 1, 2), ("own", 0, 1), ("unit", 0, 1, -1), ("unit", 1, 1, -1), ("unit", 0, 1, 1), ("unit", 2, 1, 1),
+    ("unit", 2, 2, -1), ("unit", 2, 1, -1), ("unit", 0, 2, 1), ("unit", 1, 2, 1), ("second", 2, 0), ("unit", 1, 1, 1),
+    ("unit", 1, 1, 2), ("unit", 0, 1, 2), ("unit", 2, 2, 1), ("unit", 2, 1, 2), ("unit", 0, 2, 2), ("unit", 2, 2, 2),
+    ("second", 0, -1), ("unit", 1, 2, -1), ("second", 0, 0), ("second", 1, -1), ("unit", 0, 2, -1), ("second", 0, 1),
+    ("second", 1, 0), ("second", 2, 1), ("second", 2, -1), ("second", 1, 1), ("unit", 1, 2, 2), ("second", 1, 2),
+    ("row", 1, -1), ("second", 0, 2), ("row", 0, -1), ("row", 2, -1), ("row", 2, 1), ("row", 0, 1), ("second", 2, 2),
+    ("row", 1, 1), ("third", 1, 0), ("row", 1, 2), ("row", 2, 2), ("row", 0, 2), ("third", 2, 0), ("third", 0, 0),
+    ("mul", 0), ("third", 1, 1), ("third", 2, 1), ("third", 0, 1), ("mul", 2), ("third", 0, -1), ("third", 1, -1),
+    ("third", 2, -1), ("mul", 1), ("mul", 3), ("third", 0, 2), ("third", 2, 2), ("third", 1, 2), ("mul", 4),
+    ("mul", 5), ("mul", 6), ("mul", 7),
 )
 SCATTER = (
-    ("terms", 0), ("first", 1, 2), ("terms", 1), ("first", 1, 1), ("first", 2, 2), ("first", 1, -1), ("first", 1, 0),
-    ("terms", 2), ("first", 0, 2), ("first", 0, 1), ("first", 0, -1), ("first", 0, 0), ("terms", 3), ("first", 2, 1),
-    ("terms", 4), ("first", 2, -1), ("terms", 5), ("first", 2, 0), ("row", 0, 2), ("row", 1, 2), ("row", 2, 2),
-    ("row", 0, 1), ("row", 1, 1), ("row", 2, 1), ("row", 0, -1), ("second", 0), ("row", 1, -1), ("second", 1),
-    ("row", 2, -1), ("second", 2), ("own", 0, 2), ("own", 1, 2), ("own", 2, 2), ("add", 0), ("unit", 0, 2),
-    ("unit", 0, 1), ("unit", 0, -1), ("add", 1), ("unit", 1, 2), ("unit", 1, 1), ("unit", 1, -1), ("add", 2),
-    ("unit", 2, 2), ("unit", 2, 1), ("unit", 2, -1), ("own", 0, 1), ("own", 1, 1), ("own", 2, 1), ("own", 0, -1),
-    ("own", 1, -1), ("own", 2, -1), ("third", 0), ("third", 1), ("third", 2), ("own", 0, 0), ("own", 1, 0),
-    ("own", 2, 0), ("unit", 0, 0), ("unit", 1, 0), ("unit", 2, 0), ("last", 0), ("last", 1), ("last", 2), ("end", 0),
-    ("end", 1), ("end", 2),
+    ("terms", 0), ("first", 1, 2), ("terms", 1), ("first", 2, 2), ("terms", 2), ("first", 0, -1), ("row", 1, 2),
+    ("terms", 3), ("first", 0, 1), ("first", 2, 1), ("first", 0, 2), ("first", 1, -1), ("row", 2, 2), ("first", 0, 0),
+    ("terms", 5), ("first", 1, 1), ("first", 1, 0), ("first", 2, 0), ("second", 1), ("terms", 4), ("first", 2, -1),
+    ("row", 0, 2), ("row", 1, -1), ("row", 2, 1), ("row", 1, 1), ("row", 0, 1), ("row", 0, -1), ("row", 2, -1),
+    ("second", 0), ("second", 2), ("own", 1, 1), ("own", 0, 1), ("own", 2, -1), ("own", 0, -1), ("own", 2, 2),
+    ("add", 1), ("own", 1, 2), ("own", 1, -1), ("own", 2, 1), ("add", 2), ("unit", 1, 1), ("unit", 2, -1),
+    ("unit", 1, 2), ("unit", 2, 2), ("unit", 2, 1), ("unit", 1, -1), ("add", 0), ("unit", 0, 1), ("unit", 0, 2),
+    ("own", 1, 0), ("own", 0, 2), ("unit", 0, -1), ("unit", 2, 0), ("unit", 1, 0), ("unit", 0, 0), ("last", 1),
+    ("last", 2), ("own", 0, 0), ("last", 0), ("own", 2, 0), ("end", 1), ("end", 2), ("end", 0),
 )
 
 
@@ -90,7 +89,7 @@
     gradient_out,
     act, held, grads, acc, other, factor, stage,
     old_params, old_moment, old_second, old_grad,
-    first_rows, full_rows, full_units, first_second, second_units, first_last, last_unit,
+    first_rows, full_rows, full_units, first_second, second_units, last_units,
     final, finals, send_sems, recv_sems, local_sems,
 ):
     outer = lax.axis_index("outer")
@@ -105,7 +104,7 @@
         place[axis] = ring(place[axis], way)
         return device(*place, core)
 
-    neighbours = {(axis, way): neighbour(axis, way) for axis in range(3) for way in WAYS}
+    neighbours = {(axis, way): neighbour(axis, way) for axis in range(3) for way in (1, -1, 2)}
     sibling = device(*own, 1 - core)
 
     barrier = pltpu.get_barrier_semaphore()
@@ -139,11 +138,11 @@
     seen = set()
     leaving = {
         "rows": (0, stage.at[0]),
-        "g1": (1, held.at[:, 0, 0, 0:3]), "g1f": (1,), "g2": (2, held.at[:, 0, 0:3]), "g2f": (2,),
+        "g1": (1, held.at[:, 0, 0, 0:3]), "g2": (2, held.at[:, 0, 0:3]), "g2f": (2,),
         "g3": (3, held.at[:, 0:3]), "g3r": (3,), "g3f": (3,),
         "products": (4, acc),
         "s1": (5, grads.at[:, 0:3]), "s2": (5,), "s2u": (5,), "s3": (6, grads.at[:, 0, 0:3]), "s4": (6,),
-        "s5": (7, grads.at[:, 0, 0, 0:3]), "s6": (7,),
+        "s6": (7, grads.at[:, 0, 0, 0:3]),
         "end": (8, finals),
     }
 
@@ -157,9 +156,7 @@
             return (name, key[3]), held.at[:, 0, 0]
         ref = held if name[0] == "g" else grads
         if name in ("g1", "s6"):
-            return (name, p), ref.at[p, 0, 0, 0:2]
-        if name in ("g1f", "s5"):
-            return (name, p), ref.at[p, 0, 0, 0]
+            return (name, p), ref.at[p, 0, 0, 0:3]
         if name in ("g2f", "s3"):
             return (name, p), ref.at[p, 0, 0]
         if name == "g3":
@@ -250,17 +247,16 @@
 
     def give_own(p, level):
         one, two, three = places(p)
-        give((f"g{level + 1}",) + ((0,) if level else ()), p, level, unit(p, three, two, one))
-
-    def pass_first(p):
-        one, two, three = places(p)
-        for way in WAYS:
-            arrived(("g1", p, way))
-            pass_on(("g1f", p, way), p, 0, way, held.at[p, three, two, ring(one, -way), half(way, 64)])
+        ref = unit(p, three, two, one)
+        if level:
+            give((f"g{level + 1}", 0), p, level, ref)
+            return
+        for step in (2, 1, -1):
+            send(("g1", p, step), ref, ref, neighbours[ORDER[p][0], step])
 
     def give_unit(p, level, step):
         one, two, three = places(p)
-        arrived(("g1f" if step == 2 else "g1", p, 1))
+        arrived(("g1", p, step))
         give((f"g{level + 1}", step), p, level, unit(p, three, two, ring(one, step)))
 
     def pass_second(p, step):
@@ -317,7 +313,7 @@
             load_own(tokens).wait()
             load_sibling(tokens).wait()
         for p in range(3):
-            arrived(("g1", p, 1), ("g1f", p, 1), *[("g2", p, 1, k) for k in STEPS])
+            arrived(("g1", p, 1), *[("g2", p, 1, k) for k in STEPS])
             if which >= 3:
                 arrived(("g2f", p, 1, 0))
             for way in WAYS:
@@ -342,7 +338,7 @@
             acc[...] = part
 
     actions = {
-        "own": give_own, "first": pass_first, "unit": give_unit, "second": pass_second,
+        "own": give_own, "unit": give_unit, "second": pass_second,
         "row": give_row, "third": pass_third, "mul": multiply,
     }
     for name, *rest in GATHER:
@@ -488,44 +484,27 @@
             total += second_units[p, SIDE[way], SLOT[step]].astype(f32)
         return total
 
-    def send_third(p):
-        one, two, three = places(p)
-        grads[p, three, two, ring(one, 2)] = sum_unit(p, 2).astype(bf16)
-        for way in WAYS:
+    def send_last(p):
+        one, two, three = places(p)
+        for step in (2, 1, -1):
+            grads[p, three, two, ring(one, step)] = sum_unit(p, step).astype(bf16)
             send(
-                ("s5", p, way),
-                grads.at[p, three, two, ring(one, 2), half(way, 64)],
-                first_last.at[p, SIDE[way]],
-                neighbours[ORDER[p][0], way],
-            )
-
-    def send_last(p):
-        one, two, three = places(p)
-        for way in WAYS:
-            total = sum_unit(p, way)
-            arrived(("s5", p, way))
-            low, high = total[:32], total[32:]
-            extra = first_last[p, SIDE[way]].astype(f32)
-            low, high = (low + extra, high) if way == 1 else (low, high + extra)
-            grads[p, three, two, ring(one, way), :32] = low.astype(bf16)
-            grads[p, three, two, ring(one, way), 32:] = high.astype(bf16)
-            send(
-                ("s6", p, way),
-                grads.at[p, three, two, ring(one, way)],
-                last_unit.at[p, SIDE[way]],
-                neighbours[ORDER[p][0], way],
+                ("s6", p, step),
+                grads.at[p, three, two, ring(one, step)],
+                last_units.at[p, SLOT[step]],
+                neighbours[ORDER[p][0], step],
             )
 
     def finish(p):
         total = sum_unit(p, 0)
-        for way in WAYS:
-            arrived(("s6", p, way))
-            total += last_unit[p, SIDE[way]].astype(f32)
+        arrived(("s6", p, 2))
+        for step in (2, 1, -1):
+            total += last_units[p, SLOT[step]].astype(f32)
         final[p * 64 : p * 64 + 64] = total
 
     actions = {
         "terms": terms, "first": send_first, "row": send_row, "own": send_own_row, "second": send_second,
-        "add": add_second, "unit": send_unit, "third": send_third, "last": send_last, "end": finish,
+        "add": add_second, "unit": send_unit, "last": send_last, "end": finish,
     }
     for name, *rest in SCATTER:
         actions[name](*rest)
@@ -568,12 +547,11 @@
             pltpu.VMEM((3, 2, 4, 64, 256), bf16),
             pltpu.VMEM((3, 2, 4, 32, 256), bf16),
             pltpu.VMEM((3, 2, 4, 64, 256), bf16),
-            pltpu.VMEM((3, 2, 32, 256), bf16),
-            pltpu.VMEM((3, 2, 64, 256), bf16),
+            pltpu.VMEM((3, 3, 64, 256), bf16),
             pltpu.VMEM((192, 256), f32),
             pltpu.VMEM((96, 256), f32),
             pltpu.SemaphoreType.DMA((9,)),
-            pltpu.SemaphoreType.DMA((95,)),
+            pltpu.SemaphoreType.DMA((89,)),
             pltpu.SemaphoreType.DMA((7,)),
         ],
         compiler_params=pltpu.CompilerParams(

time: 79.7 us -> 79.3 us (level)
  no operation moved by 1% of the time
where the time goes in v4:
time: 79.3 us; the launch traced here: 79.2 us
  Pallas kernels  76.9 us (97%)
  other arithmetic  0.93 us (1%)
    pallas_call x1, Pallas kernels, per_device(): pl.pallas_call(kernel, out_shape=pltpu.VMEM(shard, f32), in_specs=[pl.Blo...  76.9 us

profile of v4, /device:TPU:1, one launch (start us, length us, event | category | flops | bytes accessed | tf_op | source)
XLA Modules:
  0.0 79.2 jit_solution(13962810982457898626)
XLA Ops:
  0.6 0.0 copy-start
  0.6 0.0 copy-start.1
  0.7 0.0 copy-start.2
  0.7 0.0 copy-start.3
  0.7 76.9 %shard_map.93 = f32[1,96,512]{2,1,0:T(8,128)S(1)} custom-call(bf16[1,96,512]{2,1,0:T(8,128)(2,1)} %params.1, bf16[1,96,512]{2,1,0:T(8,128)(2,1)} %moment.1, bf16[1,96,512]{2,1,0:T(8,128)(2,1)} %second.1, f32[1,96,512]{2,1,0:T(8,128)} %grad_prev.1, bf16[384,12288]{1,0:T(8,128)(2,1)} %tokens.1, bf16[384,12288]{1,0:T(8,128)(2,1)} %cotangent.1), custom_call_target="tpu_custom_call" | custom-call | tf_op jit(solution)/shard_map/pallas_call | solution.py:528
  77.6 0.7 copy.11
  78.3 0.0 copy-done
  78.3 0.0 copy-done.1
  78.3 0.0 copy-done.2
  78.3 0.0 copy-done.3
  78.3 0.9 %fusion.5 = (bf16[1,96,512]{2,1,0:T(8,128)(2,1)}, bf16[1,96,512]{2,1,0:T(8,128)(2,1)}, bf16[1,96,512]{2,1,0:T(8,128)(2,1)}) fusion(f32[1,96,512]{2,1,0:T(8,128)S(1)} %copy-done, bf16[1,96,512]{2,1,0:T(8,128)(2,1)S(1)} %copy-done.1, bf16[1,96,512]{2,1,0:T(8,128)(2,1)S(1)} %copy-done.2, bf16[1,96,512]{2,1,0:T(8,128)(2,1)S(1)} %copy-done.3), kind=kLoop, calls=%fused_computation.9 | loop fusion | flops 1032192 | bytes 786432 | tf_op jit(solution)/shard_map/convert_element_type | solution.py:50
Async XLA Ops:
  0.6 77.6 %copy-start = (f32[1,96,512]{2,1,0:T(8,128)S(1)}, f32[1,96,512]{2,1,0:T(8,128)}, u32[]{:S(2)}) copy-start(f32[1,96,512]{2,1,0:T(8,128)} %grad_prev.1) | copy-start | bytes 589828
  0.6 77.6 %copy-start.1 = (bf16[1,96,512]{2,1,0:T(8,128)(2,1)S(1)}, bf16[1,96,512]{2,1,0:T(8,128)(2,1)}, u32[]{:S(2)}) copy-start(bf16[1,96,512]{2,1,0:T(8,128)(2,1)} %second.1) | copy-start | bytes 294916
  0.7 77.6 %copy-start.2 = (bf16[1,96,512]{2,1,0:T(8,128)(2,1)S(1)}, bf16[1,96,512]{2,1,0:T(8,128)(2,1)}, u32[]{:S(2)}) copy-start(bf16[1,96,512]{2,1,0:T(8,128)(2,1)} %moment.1) | copy-start | bytes 294916
  0.7 77.6 %copy-start.3 = (bf16[1,96,512]{2,1,0:T(8,128)(2,1)S(1)}, bf16[1,96,512]{2,1,0:T(8,128)(2,1)}, u32[]{:S(2)}) copy-start(bf16[1,96,512]{2,1,0:T(8,128)(2,1)} %params.1) | copy-start | bytes 294916
